TPU v7x, 128 devices: a whole 4x4x4 slice. The times are simulated.
128 devices in a mesh: sp: 32 (over x, z, y_hi), ch: 4 (over y_lo, core).
Axes of the slice: x: 4, y: 4 (y_hi: 2, y_lo: 2; y = y_hi * 2 + y_lo), z: 4, core: 2. Of those that a mesh axis runs over, the one named last changes fastest.
Arguments:
- features: bfloat16 [64, 256, 1024], P('sp', 'ch'), may hold values from -6 to 6
- weight: bfloat16 [27, 256, 256], P(None, 'ch'), may hold values from -0.078125 to 0.078125
- cotangent: bfloat16 [64, 256, 1024], P('sp', 'ch'), may hold values from -6 to 6
Outputs:
- grad_input: float32 [64, 256, 1024], P('sp', 'ch')
- grad_weight: float32 [27, 256, 256], P(None, 'ch')
All inputs are finite; a program needn't handle non-finite values.
Results may differ from a plain program's by a relative error of at most 0.0029.
Values may be sent and summed in bfloat16 or wider, within the bound.
A program may use at most 128 MiB of HBM per device.

v0:
```python
import math

import jax
import jax.numpy as jnp
from jax import lax
from jax.sharding import PartitionSpec as P

HEIGHT = 32
WIDTH = 32


def with_halo(value, sides, width):
    for axis, dim in sides:
        devices, length = (lax.axis_size(axis), value.shape[dim])
        up = [(i, (i + 1) % devices) for i in range(devices - 1)]
        down = [(j, i) for i, j in up]
        last = lax.slice_in_dim(value, length - width, length, axis=dim)
        first = lax.slice_in_dim(value, 0, width, axis=dim)
        before = lax.ppermute(last, axis, up)
        after = lax.ppermute(first, axis, down)
        value = jnp.concatenate([before, value, after], axis=dim)
    return value


def spread(field):
    planes, chans, _ = field.shape
    grid = field.reshape(planes, chans, HEIGHT, WIDTH)
    return jnp.pad(grid, ((0, 0), (0, 0), (1, 1), (1, 1)))


def window(padded, shift_d, shift_h, shift_w, planes):
    piece = padded[
        shift_d : shift_d + planes, :, shift_h : shift_h + HEIGHT, shift_w : shift_w + WIDTH
    ]
    return piece.reshape(planes, padded.shape[1], HEIGHT * WIDTH)


def local(features, weight, cotangent):
    planes, quarter, _ = features.shape
    out_local = weight.shape[1]
    gathered = lax.all_gather(features, "ch", axis=1, tiled=True)
    padded = with_halo(gathered, (("sp", 0),), 1)
    padded = spread(padded)
    preact = jnp.zeros((planes, out_local, HEIGHT * WIDTH), jnp.float32)
    for stencil in range(27):
        patch = window(padded, stencil // 9, stencil // 3 % 3, stencil % 3, planes)
        preact = preact + jnp.einsum(
            "dcp,oc->dop", patch, weight[stencil], preferred_element_type=jnp.float32
        )
    sigmoid_pre = jax.nn.sigmoid(preact)
    slope = sigmoid_pre * (1.0 + preact * (1.0 - sigmoid_pre))
    grad_pre = (cotangent.astype(jnp.float32) * slope).astype(jnp.bfloat16)
    partial_grads = []
    for stencil in range(27):
        patch = window(padded, stencil // 9, stencil // 3 % 3, stencil % 3, planes)
        partial_grads.append(
            jnp.einsum("dcp,dop->oc", patch, grad_pre, preferred_element_type=jnp.float32)
        )
    total_cells = planes * HEIGHT * WIDTH * lax.axis_size("sp")
    grad_weight = lax.psum(jnp.stack(partial_grads), "sp") / math.sqrt(total_cells)
    grad_edged = with_halo(grad_pre, (("sp", 0),), 1)
    grad_pad = spread(grad_edged)
    inputs = weight.shape[2]
    summed = jnp.zeros((planes, inputs, HEIGHT * WIDTH), jnp.float32)
    for stencil in range(27):
        moved = window(grad_pad, 2 - stencil // 9, 2 - stencil // 3 % 3, 2 - stencil % 3, planes)
        summed = summed + jnp.einsum(
            "dop,oc->dcp", moved, weight[stencil], preferred_element_type=jnp.float32
        )
    grad_input = lax.psum_scatter(summed, "ch", scatter_dimension=1, tiled=True)
    return (grad_input, grad_weight)


def solution(mesh):
    placed = (P("sp", "ch", None), P(None, "ch", None), P("sp", "ch", None))
    return jax.shard_map(
        local,
        mesh=mesh,
        in_specs=placed,
        out_specs=(P("sp", "ch", None), P(None, "ch", None)),
        check_vma=False,
    )
```

profile of v0, /device:TPU:0, one launch (start us, length us, event | category | flops | bytes accessed | tf_op | source)
XLA Modules:
  0.0 551.2 jit_solution(10232937195065666312)
XLA Ops:
  7.9 24.9 %all-gather.2.cloned.1.call-done = bf16[2,256,1024]{2,1,0:T(8,128)(2,1)} async-done(((bf16[2,64,1024]{2,1,0:T(8,128)(2,1)}), bf16[2,256,1024]{2,1,0:T(8,128)(2,1)}) %all-gather.2.cloned.1.call-update) | async-done | bytes 1048592 | tf_op jit(solution)/shard_map/all_gather | solution.py:41
  34.2 4.7 collective-permute-start
  40.2 21.5 %collective-permute-done = bf16[1,256,1024]{2,1,0:T(8,128)(2,1)S(1)} collective-permute-done((bf16[1,256,1024]{2,1,0:T(8,128)(2,1)S(1)}, bf16[1,256,1024]{2,1,0:T(8,128)(2,1)S(1)}, u32[]{:S(2)}, u32[]{:S(2)}) %collective-permute-start) | collective-permute-done | bytes 524320 | tf_op jit(solution)/shard_map/ppermute | solution.py:19
  61.7 2.3 collective-permute-done.1
  66.3 2.8 copy.81
  69.1 7.4 %pad_slice_fusion.4 = (bf16[2,256,32,32]{1,3,2,0:T(8,128)(2,1)S(1)}, bf16[2,256,32,32]{1,3,2,0:T(8,128)(2,1)}, bf16[2,256,32,32]{1,3,2,0:T(8,128)(2,1)}, bf16[2,...) fusion(bf16[4,256,32,32]{1,3,2,0:T(8,128)(2,1)S(1)} %bitcast.534), kind=kLoop, calls=%fused_computation.4 | loop fusion | bytes 22020096 | tf_op jit(solution)/shard_map/slice | solution.py:32
  76.6 2.7 pad_slice_fusion.23
  121.1 6.1 %collective-permute-start.2 = (bf16[1,64,1024]{2,1,0:T(8,128)(2,1)}, bf16[1,64,1024]{2,1,0:T(8,128)(2,1)S(1)}, u32[]{:S(2)}, u32[]{:S(2)}) collective-permute-start(bf16[1,64,1024]{2,1,0:T(8,128)(2,1)} %get-tuple-element.58), channel_id=1, source_target_pairs={{0,4},{4,8},{8,12},{12,16},{16,20},{20,24},{24,28},{28,32},{32,36}... | collective-permute-start | bytes 393224 | tf_op jit(solution)/shard_map/ppermute | solution.py:19
  132.4 4.0 pad_slice_fusion.46
  137.6 1.8 fusion.100
  139.4 1.8 fusion.103
  141.2 1.8 fusion.106
  143.0 1.8 fusion.110
  151.7 1.8 fusion.130
  156.9 1.8 fusion.71
  158.7 1.8 fusion.74
  160.5 1.8 fusion.77
  162.3 1.8 fusion.80
  179.7 1.8 fusion.44
  181.5 18.9 %bitcast_add_fusion = f32[2,256,1024]{1,2,0:T(8,128)} fusion(f32[2,1024,256]{2,1,0:T(8,128)} %fusion.51, f32[2,1024,256]{2,1,0:T(8,128)} %fusion.54, f32[2,1024,256]{2,1,0:T(8,128)} %fusion.57, f32[2,1024,256]{2,1,0:T(8,128)} %fusion.60, f32[2,1024,256]{2,1,0:T(8,128)} %fusion.65, f32[2,1024,256]{2,1,0:T(8,128)} %fusion.68, f32[2,1024,256]{2,1,0:T(8,128)} %fusion.71, ...), kind=kOutput, calls=%fused_computation.25 | convolution fusion | flops 81526784 | bytes 57049088 | tf_op jit(solution)/shard_map/dop,oc->dcp/dot_general | solution.py:67
  200.4 4.2 copy.131
  206.5 279.0 %all-reduce.6.cloned.1.call-done = f32[27,64,256]{2,1,0:T(8,128)} async-done(((f32[27,64,256]{2,1,0:T(8,128)}), f32[27,64,256]{2,1,0:T(8,128)}) %all-reduce.6.cloned.1.call-update) | async-done | bytes 1769488 | tf_op jit(solution)/shard_map/psum | solution.py:60
  485.5 2.9 broadcast_multiply_fusion
  488.4 54.2 %all-reduce.8.cloned.1.call-done = f32[2,256,1024]{2,0,1:T(2,128)} async-done(((f32[2,256,1024]{2,0,1:T(2,128)}), f32[2,256,1024]{2,0,1:T(2,128)}) %all-reduce.8.cloned.1.call-update) | async-done | bytes 2097168
  (135 shorter events, 82.9 us)
Async XLA Ops:
  7.2 25.7 %all-gather.2.cloned.1.call-start = ((), (), s32[]{:S(2)}) async-start(), calls=%async_computation | async-start | bytes 1310720 | tf_op jit(solution)/shard_map/all_gather | solution.py:41
  7.9 477.6 %all-reduce.6.cloned.1.call-start = ((), (), s32[]{:S(2)}) async-start(), calls=%async_computation.1 | async-start | bytes 3538944 | tf_op jit(solution)/shard_map/psum | solution.py:60
  32.8 31.9 %copy-start = (bf16[2,256,1024]{2,1,0:T(8,128)(2,1)S(1)}, bf16[2,256,1024]{2,1,0:T(8,128)(2,1)}, u32[]{:S(2)}) copy-start(bf16[2,256,1024]{2,1,0:T(8,128)(2,1)} %all-gather.2.cloned.1.call-done) | copy-start | bytes 3145732
  34.2 27.5 %collective-permute-start = (bf16[1,256,1024]{2,1,0:T(8,128)(2,1)S(1)}, bf16[1,256,1024]{2,1,0:T(8,128)(2,1)S(1)}, u32[]{:S(2)}, u32[]{:S(2)}) collective-permute-start(bf16[1,256,1024]{2,1,0:T(8,128)(2,1)S(1)} %get-tuple-element.56), channel_id=1, source_target_pairs={{0,4},{4,8},{8,12},{12,16},{16,20},{20,24},{24,28},{28,32},{32,36}... | collective-permute-start | bytes 1572872 | tf_op jit(solution)/shard_map/ppermute | solution.py:19
  38.9 25.1 %collective-permute-start.1 = (bf16[1,256,1024]{2,1,0:T(8,128)(2,1)S(1)}, bf16[1,256,1024]{2,1,0:T(8,128)(2,1)S(1)}, u32[]{:S(2)}, u32[]{:S(2)}) collective-permute-start(bf16[1,256,1024]{2,1,0:T(8,128)(2,1)S(1)} %get-tuple-element.57), channel_id=1, source_target_pairs={{4,0},{8,4},{12,8},{16,12},{20,16},{24,20},{28,24},{32,28},{36,32}... | collective-permute-start | bytes 1572872 | tf_op jit(solution)/shard_map/ppermute | solution.py:20
  61.7 2.3 copy-start.15
  76.6 2.7 copy-start.13
  79.3 1.2 copy-start.6
  79.3 1.7 copy-start.7
  79.3 2.1 copy-start.8
  80.5 1.4 copy-start.9
  81.4 1.4 copy-start.1
  84.6 1.3 copy-start.12
  85.4 1.3 copy-start.11
  85.9 1.3 copy-start.10
  87.9 1.2 copy-start.5
  88.2 1.3 copy-start.4
  89.1 1.3 copy-start.3
  89.5 1.3 copy-start.2
  119.8 8.6 %collective-permute-start.3 = (bf16[1,64,1024]{2,1,0:T(8,128)(2,1)}, bf16[1,64,1024]{2,1,0:T(8,128)(2,1)S(1)}, u32[]{:S(2)}, u32[]{:S(2)}) collective-permute-start(bf16[1,64,1024]{2,1,0:T(8,128)(2,1)} %get-tuple-element.59), channel_id=1, source_target_pairs={{4,0},{8,4},{12,8},{16,12},{20,16},{24,20},{28,24},{32,28},{36,32}... | collective-permute-start | bytes 393224 | tf_op jit(solution)/shard_map/ppermute | solution.py:20
  121.1 8.9 %collective-permute-start.2 = (bf16[1,64,1024]{2,1,0:T(8,128)(2,1)}, bf16[1,64,1024]{2,1,0:T(8,128)(2,1)S(1)}, u32[]{:S(2)}, u32[]{:S(2)}) collective-permute-start(bf16[1,64,1024]{2,1,0:T(8,128)(2,1)} %get-tuple-element.58), channel_id=1, source_target_pairs={{0,4},{4,8},{8,12},{12,16},{16,20},{20,24},{24,28},{28,32},{32,36}... | collective-permute-start | bytes 393224 | tf_op jit(solution)/shard_map/ppermute | solution.py:19
  128.1 414.5 %all-reduce.8.cloned.1.call-start = ((), (), s32[]{:S(2)}) async-start(), calls=%async_computation.2 | async-start | bytes 4194304
  128.4 1.6 copy-start.17
  176.2 3.5 copy-start.18
  (6 other events, 5.9 us)
Sparse Core Ops, SparseCore 0:
  9.7 23.1 all-gather.1
  128.3 357.2 all-reduce.5
  488.2 54.3 all-reduce.7
where the time goes:
time: 553 us; the launch traced here: 551 us
  waiting for transfers between devices  384 us (69%)
  matrix products  100 us (18%)
  local copies, waits for them, and re-layouts  33 us (6%)
  between operations  14.7 us (3%)
  starting transfers between devices  13.4 us (2%)
    psum x1, waiting for transfers between devices, local(): lax.psum(jnp.stack(partial_grads), 'sp') / math.sqrt(total_cells)  279 us
    dot_general x27, matrix products, local(): jnp.einsum('dop,oc->dcp', moved, weight[stencil], preferred_element_type=...  63.2 us
    unnamed x4, waiting for transfers between devices  55 us
    dot_general x27, matrix products, local(): jnp.einsum('dcp,dop->oc', patch, grad_pre, preferred_element_type=jnp.flo...  25.4 us
    all_gather x1, waiting for transfers between devices, local(): gathered = lax.all_gather(features, 'ch', axis=1, tiled=True)  24.9 us
    ppermute x2, waiting for transfers between devices, with_halo(): before = lax.ppermute(last, axis, up)  23.1 us
    slice x4, local copies, waits for them, and re-layouts, window(): padded[shift_d:shift_d + planes, :, shift_h:shift_h + HEIGHT, shift_w:shi...  14.8 us
    dot_general x27, matrix products, local(): jnp.einsum('dcp,oc->dop', patch, weight[stencil], preferred_element_type=...  11.7 us
  transfers between devices with their start and end apart: 7, of which 7 were waited for; matrix products, arithmetic and copies ran while one was open for 14% of the time, Pallas kernels for 0%

commit v1 on v0

v1 whole, which is shorter than its diff:
```python
import functools

import jax
import jax.numpy as jnp
from jax import lax
from jax.experimental import pallas as pl
from jax.experimental.pallas import tpu as pltpu
from jax.sharding import PartitionSpec as P

MESH = pl.DeviceIdType.MESH
F32, BF16 = jnp.float32, jnp.bfloat16
WIDTH = 32
CELLS = 1024
QUARTER = 64
FULL = 256
STACK = 9 * QUARTER
TILE = 256
STRIDE = 640
IN_TILE, OUT_TILE, D_TILE, ROWS = 256, 256, 256, 64
ROLL = BF16
CHUNKS = ((0, 8, 2), (8, 8, 2), (16, 11, 3))
SLOTS = 28
SCALE = 1.0 / 256.0


def wrap(value, size):
    return lax.rem(value, size)


def place():
    sp, ch = lax.axis_index("sp"), lax.axis_index("ch")
    return sp, ch, lax.div(sp, 8), lax.rem(lax.div(sp, 2), 4), lax.rem(sp, 2)


def index(x, z, y):
    return x * 8 + z * 2 + y


def roll(value, shift):
    return pltpu.roll(value, shift % CELLS, 1)


def nine(value, lane, column):
    zero = jnp.zeros_like(value)
    wide = [
        jnp.where(column <= WIDTH - 2, roll(value, -1), zero),
        value,
        jnp.where(column >= 1, roll(value, 1), zero),
    ]
    out = [jnp.where(lane < CELLS - WIDTH, roll(v, -WIDTH), zero) for v in wide]
    out += wide
    out += [jnp.where(lane >= WIDTH, roll(v, WIDTH), zero) for v in wide]
    return out


def lanes(rows):
    lane = lax.broadcasted_iota(jnp.int32, (rows, CELLS), 1)
    return lane, lax.rem(lane, WIDTH)


def shift_in(value, row, rows, stacked, plane):
    lane, column = lanes(rows)
    for s, moved in enumerate(nine(value, lane, column)):
        stacked[pl.ds(plane * STRIDE + s * QUARTER + row, rows), :] = moved.astype(BF16)


def kernel(
    f_ref, cot_ref, w_ref, gi_ref, out_ref,
    planes, edge, cot, wide_in, wide_out, turned_in, turned_out, taps_out, stacked, gedge, ghalo,
    part, exact, sum_x, sum_z, got1, got2, middle, got3, dx, dsend, dgot, dsend2, dgot2,
    local_sem, send_sem, recv_sem,
):
    sp, ch, x, z, y = place()
    other = wrap(ch + 2, 4)
    twin = lax.div(ch, 2) * 2 + wrap(ch + 1, 2)
    twin_other = wrap(twin + 2, 4)
    up, down = wrap(sp + 1, 32), wrap(sp + 31, 32)

    def near(dx_, dz_, dy_):
        return index(wrap(x + dx_, 4), wrap(z + dz_, 4), wrap(y + dy_, 2))

    barrier = pltpu.get_barrier_semaphore()
    friends = [(sp, twin), (sp, other), (up, ch), (down, ch), (up, other), (down, other)]
    friends += [(near(d, 0, 0), ch) for d in (1, 2, 3)] + [(near(0, d, 0), ch) for d in (1, 2, 3)]
    friends.append((near(0, 0, 1), ch))
    for friend in friends:
        pl.semaphore_signal(barrier, inc=1, device_id=friend, device_id_type=MESH)

    own = pl.ds(1, 2)
    mine = pl.ds(pl.multiple_of(ch * QUARTER, QUARTER), QUARTER)
    others = pl.ds(pl.multiple_of(other * QUARTER, QUARTER), QUARTER)
    twins = pl.ds(pl.multiple_of(twin * QUARTER, QUARTER), QUARTER)
    twin_others = pl.ds(pl.multiple_of(twin_other * QUARTER, QUARTER), QUARTER)

    loads = [(f_ref, planes.at[own, mine])]
    low, high = pl.ds(0, STACK), pl.ds(STACK, STACK)
    left, right = pl.ds(0, FULL), pl.ds(FULL, FULL)
    loads += [(w_ref.at[1], wide_in.at[low, left]), (w_ref.at[2], wide_in.at[low, right])]
    loads += [(w_ref.at[0], wide_in.at[high, left]), (w_ref.at[1], wide_in.at[high, right])]
    loads += [(w_ref.at[0], wide_out.at[0]), (w_ref.at[2], wide_out.at[1]), (cot_ref, cot)]
    loads = [pltpu.make_async_copy(src, dst, local_sem.at[i]) for i, (src, dst) in enumerate(loads)]
    for load in loads:
        load.start()
    loads[0].wait()
    for e, plane, inside in ((0, 2, sp < 31), (1, 1, sp > 0)):
        value = planes[plane, mine, :]
        edge[e] = jnp.where(inside, value, jnp.zeros_like(value))
    pl.semaphore_wait(barrier, len(friends))

    sent = []

    def go(src, dst, device, lands):
        i = len(sent)

        def copy_to(ref):
            return pltpu.make_async_remote_copy(
                src_ref=src, dst_ref=ref, send_sem=send_sem.at[i], recv_sem=recv_sem.at[i],
                device_id=device, device_id_type=MESH,
            )

        copy = copy_to(dst)
        copy.start()
        sent.append(copy)
        return copy_to(lands)

    mine_own = planes.at[own, mine]
    across = go(mine_own, mine_own, (sp, other), planes.at[own, others])
    beside = go(mine_own, mine_own, (sp, twin), planes.at[own, twins])

    def halos(core, rows):
        out = []
        for e, peer, slot in ((0, up, 0), (1, down, 3)):
            out.append((slot, go(edge.at[e], planes.at[slot, mine], (peer, core), planes.at[slot, rows])))
        return out

    def passing(landings, rows, arriving):
        out = []
        for slot, landing in landings:
            landing.wait_recv()
            out.append(go(planes.at[slot, rows], planes.at[slot, rows], (sp, twin), planes.at[slot, arriving]))
        return out

    halo_mine = halos(ch, mine)
    halo_other = halos(other, others)

    for load in loads[1:]:
        load.wait()
    for p in range(4):
        stacked[pl.ds(p * STRIDE + STACK, STRIDE - STACK), :] = jnp.zeros((STRIDE - STACK, CELLS), BF16)
    pad = jnp.zeros((FULL, STRIDE - STACK), BF16)
    for a, src, places in (
        (0, wide_out.at[0], (turned_in.at[0, :, pl.ds(STRIDE, STRIDE)], turned_out.at[1])),
        (1, wide_in.at[low, left], (turned_in.at[0, :, pl.ds(0, STRIDE)], turned_in.at[1, :, pl.ds(STRIDE, STRIDE)])),
        (2, wide_out.at[1], (turned_in.at[1, :, pl.ds(0, STRIDE)], turned_out.at[0])),
    ):
        for k in range(0, STACK, 128):
            n = min(128, STACK - k)
            block = src[pl.ds(k, n), :].T
            for dst in places:
                dst[:, pl.ds(k, n)] = block
        for dst in places:
            dst[:, pl.ds(STACK, STRIDE - STACK)] = pad

    across.wait_recv()
    passed = go(planes.at[own, others], planes.at[own, others], (sp, twin), planes.at[own, twin_others])
    passes = passing(halo_other, others, twin_others)
    beside.wait_recv()
    passed.wait_recv()

    for n in range(0, CELLS, IN_TILE):
        cols = pl.ds(n, IN_TILE)
        taps_out[:, cols] = jnp.dot(
            wide_in[...], planes[own, :, cols].reshape(2 * FULL, IN_TILE), preferred_element_type=F32
        )

    passes += passing(halo_mine, mine, twins)
    for landing in passes:
        landing.wait_recv()

    def outer(d):
        for n in range(0, CELLS, OUT_TILE):
            cols = pl.ds(n, OUT_TILE)
            taps_out[pl.ds(d * STACK, STACK), cols] += jnp.dot(
                wide_out[d], planes[3 * d, :, cols], preferred_element_type=F32
            )

    rows = ROWS

    def slope(d, inside):
        def body(o, carry):
            at = pl.multiple_of(o * rows, rows)
            lane, column = lanes(rows)

            def tap(b, c):
                return taps_out[pl.ds(d * STACK + (3 * b + c) * QUARTER + at, rows), :]

            pre = None
            for c in range(3):
                total = tap(1, c)
                total = total + jnp.where(lane >= WIDTH, roll(tap(0, c), WIDTH), 0.0)
                total = total + jnp.where(lane < CELLS - WIDTH, roll(tap(2, c), -WIDTH), 0.0)
                if c == 0:
                    total = jnp.where(column >= 1, roll(total, 1), 0.0)
                if c == 2:
                    total = jnp.where(column <= WIDTH - 2, roll(total, -1), 0.0)
                pre = total if pre is None else pre + total
            s = 1.0 / (1.0 + jnp.exp(-pre))
            grad = cot[d, pl.ds(at, rows), :].astype(F32) * (s * (1.0 + pre * (1.0 - s)))
            grad = grad.astype(BF16)
            gedge[d, pl.ds(at, rows), :] = jnp.where(inside, grad, jnp.zeros_like(grad))
            shift_in(grad.astype(ROLL), at, rows, stacked, 1 + d)
            return carry

        lax.fori_loop(0, QUARTER // rows, body, 0)

    outer(0)
    slope(0, sp > 0)
    g_down = go(gedge.at[0], ghalo.at[1], (down, ch), ghalo.at[1])
    outer(1)
    slope(1, sp < 31)
    g_up = go(gedge.at[1], ghalo.at[0], (up, ch), ghalo.at[0])

    contract = (((1,), (1,)), ((), ()))

    def wgrad(a):
        total = None
        for d in range(2):
            term = lax.dot_general(
                stacked[pl.ds((1 + d) * STRIDE, STACK), :], planes[a + d], contract,
                preferred_element_type=F32,
            )
            total = term if total is None else total + term
        exact[pl.ds(a * 9, 9)] = total.reshape(9, QUARTER, FULL)
        part[pl.ds(a * 9, 9)] = total.astype(BF16).reshape(9, QUARTER, FULL)

    line_x = [(near(d, 0, 0), wrap(x + d, 4), wrap(x + 4 - d, 4)) for d in (1, 2, 3)]
    line_z = [(near(0, d, 0), wrap(z + d, 4), wrap(z + 4 - d, 4)) for d in (1, 2, 3)]
    halves = (
        dict(slot=0, cols=pl.ds(0, 128), me=x, line=line_x, owner=z, group=line_z, total=sum_x),
        dict(slot=1, cols=pl.ds(128, 128), me=z, line=line_z, owner=x, group=line_x, total=sum_z),
    )
    mate = (near(0, 0, 1), ch)

    def tile16(i):
        return pl.ds(pl.multiple_of(i * 16, 16), 16)

    def reduce_line(chunk):
        first, taps, per = chunk
        out = []
        for h in halves:
            for j, (peer, them, _) in enumerate(h["line"]):
                dst = got1.at[h["slot"], j, pl.ds(first, taps)]
                out.append(go(part.at[pl.ds(first, taps), tile16(them), h["cols"]], dst, (peer, ch), dst))
        return out

    def reduce_group(chunk, landings):
        first, taps, per = chunk
        out = []
        for h in halves:
            for landing in landings[3 * h["slot"] : 3 * h["slot"] + 3]:
                landing.wait_recv()
            total = exact[pl.ds(first, taps), tile16(h["me"]), h["cols"]]
            for j in range(3):
                total = total + got1[h["slot"], j, pl.ds(first, taps)].astype(F32)
            h["total"][pl.ds(first, taps)] = total
            if 4 * per > taps:
                h["total"][pl.ds(first + taps, 4 * per - taps)] = jnp.zeros((4 * per - taps, 16, 128), F32)
            for j, (peer, them, _) in enumerate(h["group"]):
                dst = got2.at[h["slot"], j, pl.ds(first // 4, per)]
                out.append(go(h["total"].at[pl.ds(first + them * per, per)], dst, (peer, ch), dst))
        return out

    def reduce_mate(chunk, landings):
        first, taps, per = chunk
        out = []
        for h in halves:
            for landing in landings[3 * h["slot"] : 3 * h["slot"] + 3]:
                landing.wait_recv()
            total = h["total"][pl.ds(first + h["owner"] * per, per)]
            for j in range(3):
                total = total + got2[h["slot"], j, pl.ds(first // 4, per)]
            here = (h["slot"], pl.ds(first // 4, per))
            middle[here] = total
            out.append(go(middle.at[here], got3.at[here], mate, got3.at[here]))
        return out

    def gather_group(chunk, landings):
        first, taps, per = chunk
        out = []
        for h in halves:
            landings[h["slot"]].wait_recv()
            here = (h["slot"], pl.ds(first // 4, per))
            total = middle[here] + got3[here]
            here = (pl.ds(first + h["owner"] * per, per), tile16(h["me"]), h["cols"])
            out_ref[here] = (total * SCALE).astype(BF16)
            for peer, _, from_them in h["group"]:
                lands = out_ref.at[pl.ds(first + from_them * per, per), tile16(h["me"]), h["cols"]]
                out.append(go(out_ref.at[here], out_ref.at[here], (peer, ch), lands))
        return out

    def gather_line(chunk, landings):
        first, taps, per = chunk
        out = []
        for h in halves:
            for landing in landings[3 * h["slot"] : 3 * h["slot"] + 3]:
                landing.wait_recv()
            here = out_ref.at[pl.ds(first, taps), tile16(h["me"]), h["cols"]]
            for peer, _, from_them in h["line"]:
                lands = out_ref.at[pl.ds(first, taps), tile16(from_them), h["cols"]]
                out.append(go(here, here, (peer, ch), lands))
        return out

    lines = []
    for a, chunk in enumerate(CHUNKS):
        wgrad(a)
        lines.append(reduce_line(chunk))

    for n in range(0, CELLS, D_TILE):
        cols = pl.ds(n, D_TILE)
        value = jnp.dot(
            turned_in[...].reshape(2 * FULL, 2 * STRIDE), stacked[pl.ds(STRIDE, 2 * STRIDE), cols],
            preferred_element_type=F32,
        )
        dx[:, :, cols] = value.reshape(2, FULL, D_TILE)

    def halo_shift(d):
        def body(o, carry):
            at = pl.multiple_of(o * rows, rows)
            shift_in(ghalo[d, pl.ds(at, rows), :].astype(ROLL), at, rows, stacked, 3 * d)
            return carry

        lax.fori_loop(0, QUARTER // rows, body, 0)

    def dgrad(d):
        for n in range(0, CELLS, D_TILE):
            cols = pl.ds(n, D_TILE)
            dx[d, :, cols] += jnp.dot(
                turned_out[d], stacked[pl.ds(3 * d * STRIDE, STRIDE), cols], preferred_element_type=F32
            )

    chips, crosses = [], []

    def neighbour(d, landing):
        landing.wait_recv()
        halo_shift(d)
        dgrad(d)
        dsend[d, 0] = dx[d, twins, :].astype(BF16)
        dsend[d, 1] = dx[d, twin_others, :].astype(BF16)
        chips.append((d, go(dsend.at[d], dgot.at[d], (sp, twin), dgot.at[d])))

    def cross_over(d, chip):
        chip.wait_recv()
        dsend2[d] = (dx[d, others, :] + dgot[d, 1].astype(F32)).astype(BF16)
        crosses.append((d, go(dsend2.at[d], dgot2.at[d], (sp, other), dgot2.at[d])))

    groups = [reduce_group(chunk, line) for chunk, line in zip(CHUNKS, lines)]
    mates = [reduce_mate(CHUNKS[0], groups[0])]
    neighbour(1, g_down)
    mates.append(reduce_mate(CHUNKS[1], groups[1]))
    neighbour(0, g_up)
    mates.append(reduce_mate(CHUNKS[2], groups[2]))
    cross_over(*chips[0])
    broadcasts = [gather_group(CHUNKS[0], mates[0])]
    cross_over(*chips[1])
    broadcasts += [gather_group(chunk, mate_) for chunk, mate_ in zip(CHUNKS[1:], mates[1:])]
    finals = [gather_line(chunk, landings) for chunk, landings in zip(CHUNKS, broadcasts)]
    for d, cross in crosses:
        cross.wait_recv()
        gi_ref[d] = dx[d, mine, :] + dgot[d, 0].astype(F32) + dgot2[d].astype(F32)
    for landings in finals:
        for landing in landings:
            landing.wait_recv()
    for copy in sent:
        copy.wait_send()


COPIES = 2 + 4 + 1 + 4 + 2 + 2 + 2 + 26 * len(CHUNKS)


def local(features, weight, cotangent):
    vmem = pl.BlockSpec(memory_space=pltpu.VMEM)
    grad_input, grad_weight = pl.pallas_call(
        kernel,
        out_shape=(
            jax.ShapeDtypeStruct((2, QUARTER, CELLS), F32),
            jax.ShapeDtypeStruct((SLOTS, QUARTER, FULL), BF16),
        ),
        in_specs=[pl.BlockSpec(memory_space=pltpu.HBM)] * 3,
        out_specs=(vmem, vmem),
        scratch_shapes=[
            pltpu.VMEM((4, FULL, CELLS), BF16),
            pltpu.VMEM((2, QUARTER, CELLS), BF16),
            pltpu.VMEM((2, QUARTER, CELLS), BF16),
            pltpu.VMEM((2 * STACK, 2 * FULL), BF16),
            pltpu.VMEM((2, STACK, FULL), BF16),
            pltpu.VMEM((2, FULL, 2 * STRIDE), BF16),
            pltpu.VMEM((2, FULL, STRIDE), BF16),
            pltpu.VMEM((2 * STACK, CELLS), F32),
            pltpu.VMEM((4 * STRIDE, CELLS), BF16),
            pltpu.VMEM((2, QUARTER, CELLS), BF16),
            pltpu.VMEM((2, QUARTER, CELLS), BF16),
            pltpu.VMEM((27, QUARTER, FULL), BF16),
            pltpu.VMEM((27, QUARTER, FULL), F32),
            pltpu.VMEM((SLOTS, 16, 128), F32),
            pltpu.VMEM((SLOTS, 16, 128), F32),
            pltpu.VMEM((2, 3, 27, 16, 128), BF16),
            pltpu.VMEM((2, 3, SLOTS // 4, 16, 128), F32),
            pltpu.VMEM((2, SLOTS // 4, 16, 128), F32),
            pltpu.VMEM((2, SLOTS // 4, 16, 128), F32),
            pltpu.VMEM((2, FULL, CELLS), F32),
            pltpu.VMEM((2, 2, QUARTER, CELLS), BF16),
            pltpu.VMEM((2, 2, QUARTER, CELLS), BF16),
            pltpu.VMEM((2, QUARTER, CELLS), BF16),
            pltpu.VMEM((2, QUARTER, CELLS), BF16),
            pltpu.SemaphoreType.DMA((8,)),
            pltpu.SemaphoreType.DMA((COPIES,)),
            pltpu.SemaphoreType.DMA((COPIES,)),
        ],
        compiler_params=pltpu.CompilerParams(
            collective_id=0, has_side_effects=True, vmem_limit_bytes=62 << 20
        ),
    )(features, cotangent, weight.reshape(3, STACK, FULL))
    return grad_input, grad_weight[:27].astype(F32)


def solution(mesh):
    placed = (P("sp", "ch", None), P(None, "ch", None), P("sp", "ch", None))
    return jax.shard_map(
        local,
        mesh=mesh,
        in_specs=placed,
        out_specs=(P("sp", "ch", None), P(None, "ch", None)),
        check_vma=False,
    )
```

time: 553 us -> 58.1 us (0.11)
  waiting for transfers between devices: 384 us -> 0 us
  matrix products: 100 us -> 0 us
  Pallas kernels: 0 us -> 53.8 us
  local copies, waits for them, and re-layouts: 33 us -> 0.8 us
  between operations: 14.7 us -> 0.65 us
  starting transfers between devices: 13.4 us -> 0 us
    psum x1 -> x0, waiting for transfers between devices: 279 us -> none  [local(): lax.psum(jnp.stack(partial_grads), 'sp') / math.sqrt(total_cells)]
    dot_general x81 -> x0, matrix products: 100 us -> none  [the longest x27 63.2 us: local(): jnp.einsum('dop,oc->dcp', moved, weight[stencil], preferred_element_type=...]
    unnamed x4 -> x0, waiting for transfers between devices: 55 us -> none
    pallas_call x0 -> x1, Pallas kernels: none -> 53.8 us  [local(): pl.pallas_call(kernel, out_shape=(jax.ShapeDtypeStruct((2, QUARTER, CELLS...]
    ppermute x4 -> x0, waiting for transfers between devices: 25.6 us -> none  [the longest x2 23.1 us: with_halo(): before = lax.ppermute(last, axis, up)]
    all_gather x1 -> x0, waiting for transfers between devices: 24.9 us -> none  [local(): gathered = lax.all_gather(features, 'ch', axis=1, tiled=True)]
    slice x6 -> x0, local copies, waits for them, and re-layouts: 16.8 us -> none  [the longest x4 14.8 us: window(): padded[shift_d:shift_d + planes, :, shift_h:shift_h + HEIGHT, shift_w:shi...]
    ppermute x4 -> x0, starting transfers between devices: 13.3 us -> none  [the longest x2 10.7 us: with_halo(): before = lax.ppermute(last, axis, up)]
  transfers between devices with their start and end apart: 7 -> 0, of which waited for: 7 -> 0; matrix products, arithmetic and copies ran while one was open for 14% -> 0% of each run, Pallas kernels for 0% -> 0%
where the time goes in v1:
time: 58.1 us; the launch traced here: 57.9 us
  Pallas kernels  53.8 us (93%)
  other arithmetic  2.65 us (5%)
  local copies, waits for them, and re-layouts  0.8 us (1%)
  between operations  0.65 us (1%)
    pallas_call x1, Pallas kernels, local(): pl.pallas_call(kernel, out_shape=(jax.ShapeDtypeStruct((2, QUARTER, CELLS...  53.8 us
    convert_element_type x1, other arithmetic, local(): return (grad_input, grad_weight[:27].astype(F32))  2.65 us

profile of v1, /device:TPU:0, one launch (start us, length us, event | category | flops | bytes accessed | tf_op | source)
XLA Modules:
  0.0 57.9 jit_solution(9076879315460807636)
XLA Ops:
  0.6 53.8 %shard_map.50 = (f32[2,64,1024]{2,1,0:T(8,128)}, bf16[28,64,256]{2,1,0:T(8,128)(2,1)}) custom-call(bf16[2,64,1024]{2,1,0:T(8,128)(2,1)} %f_ref.1, bf16[2,64,1024]{2,1,0:T(8,128)(2,1)} %cot_ref.1, bf16[3,576,256]{2,1,0:T(8,128)(2,1)} %bitcast.1), custom_call_target="tpu_custom_call" | custom-call | tf_op jit(solution)/shard_map/pallas_call | solution.py:382
  54.5 0.0 copy-start
  54.5 2.7 %slice_convert_fusion = f32[27,64,256]{2,1,0:T(8,128)} fusion(bf16[28,64,256]{2,1,0:T(8,128)(2,1)} %get-tuple-element.5), kind=kLoop, calls=%fused_computation | loop fusion | flops 442368 | bytes 2654208 | tf_op jit(solution)/shard_map/convert_element_type | solution.py:423
  57.1 0.0 copy-done
  57.1 0.8 %copy.6 = f32[2,64,1024]{2,1,0:T(8,128)} copy(f32[2,64,1024]{2,1,0:T(8,128)S(1)} %copy-done) | data formatting | bytes 1048576
Async XLA Ops:
  54.5 2.7 %copy-start = (f32[2,64,1024]{2,1,0:T(8,128)S(1)}, f32[2,64,1024]{2,1,0:T(8,128)}, u32[]{:S(2)}) copy-start(f32[2,64,1024]{2,1,0:T(8,128)} %get-tuple-element.8) | copy-start | bytes 1572868

commit v2 on v1

--- a/solution.py
+++ b/solution.py
@@ -123,25 +123,20 @@
         sent.append(copy)
         return copy_to(lands)
 
-    mine_own = planes.at[own, mine]
-    across = go(mine_own, mine_own, (sp, other), planes.at[own, others])
-    beside = go(mine_own, mine_own, (sp, twin), planes.at[own, twins])
-
-    def halos(core, rows):
-        out = []
-        for e, peer, slot in ((0, up, 0), (1, down, 3)):
-            out.append((slot, go(edge.at[e], planes.at[slot, mine], (peer, core), planes.at[slot, rows])))
-        return out
-
-    def passing(landings, rows, arriving):
-        out = []
-        for slot, landing in landings:
-            landing.wait_recv()
-            out.append(go(planes.at[slot, rows], planes.at[slot, rows], (sp, twin), planes.at[slot, arriving]))
-        return out
-
-    halo_mine = halos(ch, mine)
-    halo_other = halos(other, others)
+    def cross_plane(slot):
+        return go(planes.at[slot, mine], planes.at[slot, mine], (sp, other), planes.at[slot, others])
+
+    def pass_plane(slot, rows, arriving):
+        return go(planes.at[slot, rows], planes.at[slot, rows], (sp, twin), planes.at[slot, arriving])
+
+    def halo(e, peer, slot):
+        return go(edge.at[e], planes.at[slot, mine], (peer, other), planes.at[slot, others])
+
+    across_2 = cross_plane(2)
+    halo_3 = halo(1, down, 3)
+    across_1 = cross_plane(1)
+    halo_0 = halo(0, up, 0)
+    beside = go(planes.at[own, mine], planes.at[own, mine], (sp, twin), planes.at[own, twins])
 
     for load in loads[1:]:
         load.wait()
@@ -161,11 +156,21 @@
         for dst in places:
             dst[:, pl.ds(STACK, STRIDE - STACK)] = pad
 
-    across.wait_recv()
-    passed = go(planes.at[own, others], planes.at[own, others], (sp, twin), planes.at[own, twin_others])
-    passes = passing(halo_other, others, twin_others)
+    across_2.wait_recv()
+    value = planes[2, others, :]
+    edge[2] = jnp.where(sp < 31, value, jnp.zeros_like(value))
+    late_0 = go(edge.at[2], planes.at[0, others], (up, other), planes.at[0, mine])
+    passed = [pass_plane(2, others, twin_others)]
+    halo_3.wait_recv()
+    late_3 = go(planes.at[3, others], planes.at[3, others], (sp, other), planes.at[3, mine])
+    across_1.wait_recv()
+    passed.append(pass_plane(1, others, twin_others))
+    passes = {3: [pass_plane(3, others, twin_others)]}
+    halo_0.wait_recv()
+    passes[0] = [pass_plane(0, others, twin_others)]
     beside.wait_recv()
-    passed.wait_recv()
+    for landing in passed:
+        landing.wait_recv()
 
     for n in range(0, CELLS, IN_TILE):
         cols = pl.ds(n, IN_TILE)
@@ -173,9 +178,9 @@
             wide_in[...], planes[own, :, cols].reshape(2 * FULL, IN_TILE), preferred_element_type=F32
         )
 
-    passes += passing(halo_mine, mine, twins)
-    for landing in passes:
-        landing.wait_recv()
+    for slot, late in ((0, late_0), (3, late_3)):
+        late.wait_recv()
+        passes[slot].append(pass_plane(slot, mine, twins))
 
     def outer(d):
         for n in range(0, CELLS, OUT_TILE):
@@ -213,9 +218,13 @@
 
         lax.fori_loop(0, QUARTER // rows, body, 0)
 
+    for landing in passes[0]:
+        landing.wait_recv()
     outer(0)
     slope(0, sp > 0)
     g_down = go(gedge.at[0], ghalo.at[1], (down, ch), ghalo.at[1])
+    for landing in passes[3]:
+        landing.wait_recv()
     outer(1)
     slope(1, sp < 31)
     g_up = go(gedge.at[1], ghalo.at[0], (up, ch), ghalo.at[0])
@@ -311,9 +320,10 @@
         return out
 
     lines = []
-    for a, chunk in enumerate(CHUNKS):
+    for a in range(3):
         wgrad(a)
-        lines.append(reduce_line(chunk))
+        while len(lines) < len(CHUNKS) and sum(CHUNKS[len(lines)][:2]) <= 9 * a + 9:
+            lines.append(reduce_line(CHUNKS[len(lines)]))
 
     for n in range(0, CELLS, D_TILE):
         cols = pl.ds(n, D_TILE)
@@ -354,11 +364,12 @@
         crosses.append((d, go(dsend2.at[d], dgot2.at[d], (sp, other), dgot2.at[d])))
 
     groups = [reduce_group(chunk, line) for chunk, line in zip(CHUNKS, lines)]
-    mates = [reduce_mate(CHUNKS[0], groups[0])]
+    n = len(CHUNKS)
+    mates = [reduce_mate(CHUNKS[i], groups[i]) for i in range((n + 1) // 3)]
     neighbour(1, g_down)
-    mates.append(reduce_mate(CHUNKS[1], groups[1]))
+    mates += [reduce_mate(CHUNKS[i], groups[i]) for i in range(len(mates), n - 1)]
     neighbour(0, g_up)
-    mates.append(reduce_mate(CHUNKS[2], groups[2]))
+    mates += [reduce_mate(CHUNKS[i], groups[i]) for i in range(len(mates), n)]
     cross_over(*chips[0])
     broadcasts = [gather_group(CHUNKS[0], mates[0])]
     cross_over(*chips[1])
@@ -374,7 +385,7 @@
         copy.wait_send()
 
 
-COPIES = 2 + 4 + 1 + 4 + 2 + 2 + 2 + 26 * len(CHUNKS)
+COPIES = 5 + 2 + 6 + 2 + 2 + 2 + 26 * len(CHUNKS)
 
 
 def local(features, weight, cotangent):
@@ -389,7 +400,7 @@
         out_specs=(vmem, vmem),
         scratch_shapes=[
             pltpu.VMEM((4, FULL, CELLS), BF16),
-            pltpu.VMEM((2, QUARTER, CELLS), BF16),
+            pltpu.VMEM((3, QUARTER, CELLS), BF16),
             pltpu.VMEM((2, QUARTER, CELLS), BF16),
             pltpu.VMEM((2 * STACK, 2 * FULL), BF16),
             pltpu.VMEM((2, STACK, FULL), BF16),
@@ -417,9 +428,9 @@
             pltpu.SemaphoreType.DMA((COPIES,)),
         ],
         compiler_params=pltpu.CompilerParams(
-            collective_id=0, has_side_effects=True, vmem_limit_bytes=62 << 20
+            collective_id=0, has_side_effects=True, vmem_limit_bytes=48 << 20
         ),
-    )(features, cotangent, weight.reshape(3, STACK, FULL))
+    )(*(pltpu.with_memory_space_constraint(v, pltpu.HBM) for v in (features, cotangent, weight.reshape(3, STACK, FULL))))
     return grad_input, grad_weight[:27].astype(F32)
 
 

time: 58.1 us -> 54.4 us (0.936)
  Pallas kernels: 53.8 us -> 51.4 us
  other arithmetic: 2.65 us -> 1.43 us
    pallas_call x1, Pallas kernels: 53.8 us -> 51.4 us  [local(): pl.pallas_call(kernel, out_shape=(jax.ShapeDtypeStruct((2, QUARTER, CELLS...]
    convert_element_type x1, other arithmetic: 2.65 us -> 1.43 us  [local(): return (grad_input, grad_weight[:27].astype(F32))]
where the time goes in v2:
time: 54.4 us; the launch traced here: 54.2 us
  Pallas kernels  51.4 us (94%)
  other arithmetic  1.43 us (3%)
  local copies, waits for them, and re-layouts  0.79 us (1%)
  between operations  0.64 us (1%)
    pallas_call x1, Pallas kernels, local(): pl.pallas_call(kernel, out_shape=(jax.ShapeDtypeStruct((2, QUARTER, CELLS...  51.4 us
    convert_element_type x1, other arithmetic, local(): return (grad_input, grad_weight[:27].astype(F32))  1.43 us

profile of v2, /device:TPU:0, one launch (start us, length us, event | category | flops | bytes accessed | tf_op | source)
XLA Modules:
  0.0 54.2 jit_solution(8149345927252974202)
XLA Ops:
  0.6 51.4 %shard_map.50 = (f32[2,64,1024]{2,1,0:T(8,128)S(1)}, bf16[28,64,256]{2,1,0:T(8,128)(2,1)S(1)}) custom-call(bf16[2,64,1024]{2,1,0:T(8,128)(2,1)} %f_ref.1, bf16[2,64,1024]{2,1,0:T(8,128)(2,1)} %cot_ref.1, bf16[3,576,256]{2,1,0:T(8,128)(2,1)} %bitcast.1), custom_call_target="tpu_custom_call" | custom-call | tf_op jit(solution)/shard_map/pallas_call | solution.py:393
  52.0 1.4 %slice_convert_fusion = f32[27,64,256]{2,1,0:T(8,128)} fusion(bf16[28,64,256]{2,1,0:T(8,128)(2,1)S(1)} %get-tuple-element.5), kind=kLoop, calls=%fused_computation | loop fusion | flops 442368 | bytes 2654208 | tf_op jit(solution)/shard_map/convert_element_type | solution.py:434
  53.5 0.8 %copy.6 = f32[2,64,1024]{2,1,0:T(8,128)} copy(f32[2,64,1024]{2,1,0:T(8,128)S(1)} %get-tuple-element.8) | data formatting | bytes 1048576

commit v3 on v2

--- a/solution.py
+++ b/solution.py
@@ -14,6 +14,7 @@
 QUARTER = 64
 FULL = 256
 STACK = 9 * QUARTER
+BAND = 3 * QUARTER
 TILE = 256
 STRIDE = 640
 IN_TILE, OUT_TILE, D_TILE, ROWS = 256, 256, 256, 64
@@ -66,10 +67,11 @@
 
 def kernel(
     f_ref, cot_ref, w_ref, gi_ref, out_ref,
-    planes, edge, cot, wide_in, wide_out, turned_in, turned_out, taps_out, stacked, gedge, ghalo,
+    high, edge, cot, wide_in, wide_out, turned_in, turned_out, taps_out, stacked, gedge, ghalo,
     part, exact, sum_x, sum_z, got1, got2, middle, got3, dx, dsend, dgot, dsend2, dgot2,
     local_sem, send_sem, recv_sem,
 ):
+    planes = high.at[1]
     sp, ch, x, z, y = place()
     other = wrap(ch + 2, 4)
     twin = lax.div(ch, 2) * 2 + wrap(ch + 1, 2)
@@ -92,12 +94,14 @@
     twins = pl.ds(pl.multiple_of(twin * QUARTER, QUARTER), QUARTER)
     twin_others = pl.ds(pl.multiple_of(twin_other * QUARTER, QUARTER), QUARTER)
 
-    loads = [(f_ref, planes.at[own, mine])]
-    low, high = pl.ds(0, STACK), pl.ds(STACK, STACK)
-    left, right = pl.ds(0, FULL), pl.ds(FULL, FULL)
-    loads += [(w_ref.at[1], wide_in.at[low, left]), (w_ref.at[2], wide_in.at[low, right])]
-    loads += [(w_ref.at[0], wide_in.at[high, left]), (w_ref.at[1], wide_in.at[high, right])]
-    loads += [(w_ref.at[0], wide_out.at[0]), (w_ref.at[2], wide_out.at[1]), (cot_ref, cot)]
+    loads = [(f_ref, planes.at[own, mine]), (cot_ref, cot)]
+    for b in range(3):
+        rows_b = pl.ds(b * BAND, BAND)
+        for d in range(2):
+            for p in range(2):
+                place_in = wide_in.at[pl.ds(d * BAND, BAND), pl.ds((2 * b + p) * FULL, FULL)]
+                loads.append((w_ref.at[p + 1 - d, rows_b], place_in))
+            loads.append((w_ref.at[2 * d, rows_b], wide_out.at[d, :, pl.ds(b * FULL, FULL)]))
     loads = [pltpu.make_async_copy(src, dst, local_sem.at[i]) for i, (src, dst) in enumerate(loads)]
     for load in loads:
         load.start()
@@ -105,6 +109,14 @@
     for e, plane, inside in ((0, 2, sp < 31), (1, 1, sp > 0)):
         value = planes[plane, mine, :]
         edge[e] = jnp.where(inside, value, jnp.zeros_like(value))
+
+    def shift_rows(slot, rows):
+        value = planes[slot, rows, :]
+        lane, _ = lanes(QUARTER)
+        zero = jnp.zeros_like(value)
+        high[0, slot, rows, :] = jnp.where(lane >= WIDTH, roll(value, WIDTH), zero)
+        high[2, slot, rows, :] = jnp.where(lane < CELLS - WIDTH, roll(value, -WIDTH), zero)
+
     pl.semaphore_wait(barrier, len(friends))
 
     sent = []
@@ -143,18 +155,23 @@
     for p in range(4):
         stacked[pl.ds(p * STRIDE + STACK, STRIDE - STACK), :] = jnp.zeros((STRIDE - STACK, CELLS), BF16)
     pad = jnp.zeros((FULL, STRIDE - STACK), BF16)
-    for a, src, places in (
-        (0, wide_out.at[0], (turned_in.at[0, :, pl.ds(STRIDE, STRIDE)], turned_out.at[1])),
-        (1, wide_in.at[low, left], (turned_in.at[0, :, pl.ds(0, STRIDE)], turned_in.at[1, :, pl.ds(STRIDE, STRIDE)])),
-        (2, wide_out.at[1], (turned_in.at[1, :, pl.ds(0, STRIDE)], turned_out.at[0])),
+    for a, places in (
+        (0, (turned_in.at[0, :, pl.ds(STRIDE, STRIDE)], turned_out.at[1])),
+        (1, (turned_in.at[0, :, pl.ds(0, STRIDE)], turned_in.at[1, :, pl.ds(STRIDE, STRIDE)])),
+        (2, (turned_in.at[1, :, pl.ds(0, STRIDE)], turned_out.at[0])),
     ):
-        for k in range(0, STACK, 128):
-            n = min(128, STACK - k)
-            block = src[pl.ds(k, n), :].T
+        for s in range(9):
+            b, rows_c = s // 3, pl.ds(s % 3 * QUARTER, QUARTER)
+            if a == 1:
+                block = wide_in[rows_c, pl.ds(2 * b * FULL, FULL)].T
+            else:
+                block = wide_out[a // 2, rows_c, pl.ds(b * FULL, FULL)].T
             for dst in places:
-                dst[:, pl.ds(k, n)] = block
+                dst[:, pl.ds(s * QUARTER, QUARTER)] = block
         for dst in places:
             dst[:, pl.ds(STACK, STRIDE - STACK)] = pad
+    for slot in (1, 2):
+        shift_rows(slot, mine)
 
     across_2.wait_recv()
     value = planes[2, others, :]
@@ -168,26 +185,33 @@
     passes = {3: [pass_plane(3, others, twin_others)]}
     halo_0.wait_recv()
     passes[0] = [pass_plane(0, others, twin_others)]
+    for slot in (2, 1, 3, 0):
+        shift_rows(slot, others)
     beside.wait_recv()
-    for landing in passed:
+    for slot in (1, 2):
+        shift_rows(slot, twins)
+    for slot, landing in zip((2, 1), passed):
         landing.wait_recv()
+        shift_rows(slot, twin_others)
 
     for n in range(0, CELLS, IN_TILE):
         cols = pl.ds(n, IN_TILE)
-        taps_out[:, cols] = jnp.dot(
-            wide_in[...], planes[own, :, cols].reshape(2 * FULL, IN_TILE), preferred_element_type=F32
-        )
+        value = jnp.concatenate([high[b, own, :, cols].reshape(2 * FULL, IN_TILE) for b in range(3)], axis=0)
+        taps_out[:, cols] = jnp.dot(wide_in[...], value, preferred_element_type=F32)
+    for slot in (3, 0):
+        passes[slot][0].wait_recv()
+        shift_rows(slot, twin_others)
 
     for slot, late in ((0, late_0), (3, late_3)):
         late.wait_recv()
         passes[slot].append(pass_plane(slot, mine, twins))
+        shift_rows(slot, mine)
 
     def outer(d):
         for n in range(0, CELLS, OUT_TILE):
             cols = pl.ds(n, OUT_TILE)
-            taps_out[pl.ds(d * STACK, STACK), cols] += jnp.dot(
-                wide_out[d], planes[3 * d, :, cols], preferred_element_type=F32
-            )
+            value = high[:, 3 * d, :, cols].reshape(3 * FULL, OUT_TILE)
+            taps_out[pl.ds(d * BAND, BAND), cols] += jnp.dot(wide_out[d], value, preferred_element_type=F32)
 
     rows = ROWS
 
@@ -196,19 +220,12 @@
             at = pl.multiple_of(o * rows, rows)
             lane, column = lanes(rows)
 
-            def tap(b, c):
-                return taps_out[pl.ds(d * STACK + (3 * b + c) * QUARTER + at, rows), :]
-
-            pre = None
-            for c in range(3):
-                total = tap(1, c)
-                total = total + jnp.where(lane >= WIDTH, roll(tap(0, c), WIDTH), 0.0)
-                total = total + jnp.where(lane < CELLS - WIDTH, roll(tap(2, c), -WIDTH), 0.0)
-                if c == 0:
-                    total = jnp.where(column >= 1, roll(total, 1), 0.0)
-                if c == 2:
-                    total = jnp.where(column <= WIDTH - 2, roll(total, -1), 0.0)
-                pre = total if pre is None else pre + total
+            def tap(c):
+                return taps_out[pl.ds(d * BAND + c * QUARTER + at, rows), :]
+
+            pre = tap(1)
+            pre = pre + jnp.where(column >= 1, roll(tap(0), 1), 0.0)
+            pre = pre + jnp.where(column <= WIDTH - 2, roll(tap(2), -1), 0.0)
             s = 1.0 / (1.0 + jnp.exp(-pre))
             grad = cot[d, pl.ds(at, rows), :].astype(F32) * (s * (1.0 + pre * (1.0 - s)))
             grad = grad.astype(BF16)
@@ -218,13 +235,13 @@
 
         lax.fori_loop(0, QUARTER // rows, body, 0)
 
-    for landing in passes[0]:
-        landing.wait_recv()
+    passes[0][1].wait_recv()
+    shift_rows(0, twins)
     outer(0)
     slope(0, sp > 0)
     g_down = go(gedge.at[0], ghalo.at[1], (down, ch), ghalo.at[1])
-    for landing in passes[3]:
-        landing.wait_recv()
+    passes[3][1].wait_recv()
+    shift_rows(3, twins)
     outer(1)
     slope(1, sp < 31)
     g_up = go(gedge.at[1], ghalo.at[0], (up, ch), ghalo.at[0])
@@ -242,8 +259,8 @@
         exact[pl.ds(a * 9, 9)] = total.reshape(9, QUARTER, FULL)
         part[pl.ds(a * 9, 9)] = total.astype(BF16).reshape(9, QUARTER, FULL)
 
-    line_x = [(near(d, 0, 0), wrap(x + d, 4), wrap(x + 4 - d, 4)) for d in (1, 2, 3)]
-    line_z = [(near(0, d, 0), wrap(z + d, 4), wrap(z + 4 - d, 4)) for d in (1, 2, 3)]
+    line_x = [(near(d, 0, 0), wrap(x + d, 4), wrap(x + 4 - d, 4)) for d in (2, 1, 3)]
+    line_z = [(near(0, d, 0), wrap(z + d, 4), wrap(z + 4 - d, 4)) for d in (2, 1, 3)]
     halves = (
         dict(slot=0, cols=pl.ds(0, 128), me=x, line=line_x, owner=z, group=line_z, total=sum_x),
         dict(slot=1, cols=pl.ds(128, 128), me=z, line=line_z, owner=x, group=line_x, total=sum_z),
@@ -399,14 +416,14 @@
         in_specs=[pl.BlockSpec(memory_space=pltpu.HBM)] * 3,
         out_specs=(vmem, vmem),
         scratch_shapes=[
-            pltpu.VMEM((4, FULL, CELLS), BF16),
+            pltpu.VMEM((3, 4, FULL, CELLS), BF16),
             pltpu.VMEM((3, QUARTER, CELLS), BF16),
             pltpu.VMEM((2, QUARTER, CELLS), BF16),
-            pltpu.VMEM((2 * STACK, 2 * FULL), BF16),
-            pltpu.VMEM((2, STACK, FULL), BF16),
+            pltpu.VMEM((2 * BAND, 6 * FULL), BF16),
+            pltpu.VMEM((2, BAND, 3 * FULL), BF16),
             pltpu.VMEM((2, FULL, 2 * STRIDE), BF16),
             pltpu.VMEM((2, FULL, STRIDE), BF16),
-            pltpu.VMEM((2 * STACK, CELLS), F32),
+            pltpu.VMEM((2 * BAND, CELLS), F32),
             pltpu.VMEM((4 * STRIDE, CELLS), BF16),
             pltpu.VMEM((2, QUARTER, CELLS), BF16),
             pltpu.VMEM((2, QUARTER, CELLS), BF16),
@@ -423,7 +440,7 @@
             pltpu.VMEM((2, 2, QUARTER, CELLS), BF16),
             pltpu.VMEM((2, QUARTER, CELLS), BF16),
             pltpu.VMEM((2, QUARTER, CELLS), BF16),
-            pltpu.SemaphoreType.DMA((8,)),
+            pltpu.SemaphoreType.DMA((20,)),
             pltpu.SemaphoreType.DMA((COPIES,)),
             pltpu.SemaphoreType.DMA((COPIES,)),
         ],

time: 54.4 us -> 54 us (level)
  no operation moved by 1% of the time
where the time goes in v3:
time: 54 us; the launch traced here: 53.9 us
  Pallas kernels  51 us (94%)
  other arithmetic  1.43 us (3%)
  local copies, waits for them, and re-layouts  0.79 us (1%)
  between operations  0.64 us (1%)
    pallas_call x1, Pallas kernels, local(): pl.pallas_call(kernel, out_shape=(jax.ShapeDtypeStruct((2, QUARTER, CELLS...  51 us
    convert_element_type x1, other arithmetic, local(): return (grad_input, grad_weight[:27].astype(F32))  1.43 us

profile of v3, /device:TPU:0, one launch (start us, length us, event | category | flops | bytes accessed | tf_op | source)
XLA Modules:
  0.0 53.9 jit_solution(10501757188515004268)
XLA Ops:
  0.6 51.0 %shard_map.50 = (f32[2,64,1024]{2,1,0:T(8,128)S(1)}, bf16[28,64,256]{2,1,0:T(8,128)(2,1)S(1)}) custom-call(bf16[2,64,1024]{2,1,0:T(8,128)(2,1)} %f_ref.1, bf16[2,64,1024]{2,1,0:T(8,128)(2,1)} %cot_ref.1, bf16[3,576,256]{2,1,0:T(8,128)(2,1)} %bitcast.1), custom_call_target="tpu_custom_call" | custom-call | tf_op jit(solution)/shard_map/pallas_call | solution.py:410
  51.6 1.4 %slice_convert_fusion = f32[27,64,256]{2,1,0:T(8,128)} fusion(bf16[28,64,256]{2,1,0:T(8,128)(2,1)S(1)} %get-tuple-element.5), kind=kLoop, calls=%fused_computation | loop fusion | flops 442368 | bytes 2654208 | tf_op jit(solution)/shard_map/convert_element_type | solution.py:451
  53.1 0.8 %copy.6 = f32[2,64,1024]{2,1,0:T(8,128)} copy(f32[2,64,1024]{2,1,0:T(8,128)S(1)} %get-tuple-element.8) | data formatting | bytes 1048576

commit v4 on v3

--- a/solution.py
+++ b/solution.py
@@ -12,6 +12,7 @@
 WIDTH = 32
 CELLS = 1024
 QUARTER = 64
+HALF = 32
 FULL = 256
 STACK = 9 * QUARTER
 BAND = 3 * QUARTER
@@ -135,17 +136,30 @@
         sent.append(copy)
         return copy_to(lands)
 
+    def half(quarter, k):
+        return pl.ds(pl.multiple_of(quarter * QUARTER + k * HALF, HALF), HALF)
+
     def cross_plane(slot):
         return go(planes.at[slot, mine], planes.at[slot, mine], (sp, other), planes.at[slot, others])
 
+    def cross_half(slot, k):
+        here = planes.at[slot, half(ch, k)]
+        return go(here, here, (sp, other), planes.at[slot, half(other, k)])
+
+    def halo_half(e, peer, slot, k):
+        src = edge.at[e, pl.ds(k * HALF, HALF)]
+        return go(src, planes.at[slot, half(ch, k)], (peer, other), planes.at[slot, half(other, k)])
+
     def pass_plane(slot, rows, arriving):
         return go(planes.at[slot, rows], planes.at[slot, rows], (sp, twin), planes.at[slot, arriving])
 
     def halo(e, peer, slot):
         return go(edge.at[e], planes.at[slot, mine], (peer, other), planes.at[slot, others])
 
-    across_2 = cross_plane(2)
-    halo_3 = halo(1, down, 3)
+    across_2, halo_3 = [], []
+    for k in range(2):
+        across_2.append(cross_half(2, k))
+        halo_3.append(halo_half(1, down, 3, k))
     across_1 = cross_plane(1)
     halo_0 = halo(0, up, 0)
     beside = go(planes.at[own, mine], planes.at[own, mine], (sp, twin), planes.at[own, twins])
@@ -173,13 +187,17 @@
     for slot in (1, 2):
         shift_rows(slot, mine)
 
-    across_2.wait_recv()
-    value = planes[2, others, :]
-    edge[2] = jnp.where(sp < 31, value, jnp.zeros_like(value))
-    late_0 = go(edge.at[2], planes.at[0, others], (up, other), planes.at[0, mine])
+    late_0, late_3 = [], []
+    for k in range(2):
+        strip = pl.ds(k * HALF, HALF)
+        across_2[k].wait_recv()
+        value = planes[2, half(other, k), :]
+        edge[2, strip] = jnp.where(sp < 31, value, jnp.zeros_like(value))
+        late_0.append(go(edge.at[2, strip], planes.at[0, half(other, k)], (up, other), planes.at[0, half(ch, k)]))
+        halo_3[k].wait_recv()
+        here = planes.at[3, half(other, k)]
+        late_3.append(go(here, here, (sp, other), planes.at[3, half(ch, k)]))
     passed = [pass_plane(2, others, twin_others)]
-    halo_3.wait_recv()
-    late_3 = go(planes.at[3, others], planes.at[3, others], (sp, other), planes.at[3, mine])
     across_1.wait_recv()
     passed.append(pass_plane(1, others, twin_others))
     passes = {3: [pass_plane(3, others, twin_others)]}
@@ -203,8 +221,10 @@
         shift_rows(slot, twin_others)
 
     for slot, late in ((0, late_0), (3, late_3)):
-        late.wait_recv()
-        passes[slot].append(pass_plane(slot, mine, twins))
+        for k in range(2):
+            late[k].wait_recv()
+            here = planes.at[slot, half(ch, k)]
+            passes[slot].append(go(here, here, (sp, twin), planes.at[slot, half(twin, k)]))
         shift_rows(slot, mine)
 
     def outer(d):
@@ -235,12 +255,14 @@
 
         lax.fori_loop(0, QUARTER // rows, body, 0)
 
-    passes[0][1].wait_recv()
+    for landing in passes[0][1:]:
+        landing.wait_recv()
     shift_rows(0, twins)
     outer(0)
     slope(0, sp > 0)
     g_down = go(gedge.at[0], ghalo.at[1], (down, ch), ghalo.at[1])
-    passes[3][1].wait_recv()
+    for landing in passes[3][1:]:
+        landing.wait_recv()
     shift_rows(3, twins)
     outer(1)
     slope(1, sp < 31)
@@ -402,7 +424,7 @@
         copy.wait_send()
 
 
-COPIES = 5 + 2 + 6 + 2 + 2 + 2 + 26 * len(CHUNKS)
+COPIES = 7 + 4 + 8 + 2 + 2 + 2 + 26 * len(CHUNKS)
 
 
 def local(features, weight, cotangent):

time: 54 us -> 54.9 us (1.017)
  Pallas kernels: 51 us -> 51.9 us
    pallas_call x1, Pallas kernels: 51 us -> 51.9 us  [local(): pl.pallas_call(kernel, out_shape=(jax.ShapeDtypeStruct((2, QUARTER, CELLS...]
where the time goes in v4:
time: 54.9 us; the launch traced here: 54.8 us
  Pallas kernels  51.9 us (95%)
  other arithmetic  1.43 us (3%)
  local copies, waits for them, and re-layouts  0.79 us (1%)
  between operations  0.64 us (1%)
    pallas_call x1, Pallas kernels, local(): pl.pallas_call(kernel, out_shape=(jax.ShapeDtypeStruct((2, QUARTER, CELLS...  51.9 us
    convert_element_type x1, other arithmetic, local(): return (grad_input, grad_weight[:27].astype(F32))  1.43 us

profile of v4, /device:TPU:0, one launch (start us, length us, event | category | flops | bytes accessed | tf_op | source)
XLA Modules:
  0.0 54.8 jit_solution(12589641073241921886)
XLA Ops:
  0.6 51.9 %shard_map.50 = (f32[2,64,1024]{2,1,0:T(8,128)S(1)}, bf16[28,64,256]{2,1,0:T(8,128)(2,1)S(1)}) custom-call(bf16[2,64,1024]{2,1,0:T(8,128)(2,1)} %f_ref.1, bf16[2,64,1024]{2,1,0:T(8,128)(2,1)} %cot_ref.1, bf16[3,576,256]{2,1,0:T(8,128)(2,1)} %bitcast.1), custom_call_target="tpu_custom_call" | custom-call | tf_op jit(solution)/shard_map/pallas_call | solution.py:432
  52.6 1.4 %slice_convert_fusion = f32[27,64,256]{2,1,0:T(8,128)} fusion(bf16[28,64,256]{2,1,0:T(8,128)(2,1)S(1)} %get-tuple-element.5), kind=kLoop, calls=%fused_computation | loop fusion | flops 442368 | bytes 2654208 | tf_op jit(solution)/shard_map/convert_element_type | solution.py:473
  54.0 0.8 %copy.6 = f32[2,64,1024]{2,1,0:T(8,128)} copy(f32[2,64,1024]{2,1,0:T(8,128)S(1)} %get-tuple-element.8) | data formatting | bytes 1048576

commit v5 on v3

--- a/solution.py
+++ b/solution.py
@@ -146,8 +146,6 @@
 
     across_2 = cross_plane(2)
     halo_3 = halo(1, down, 3)
-    across_1 = cross_plane(1)
-    halo_0 = halo(0, up, 0)
     beside = go(planes.at[own, mine], planes.at[own, mine], (sp, twin), planes.at[own, twins])
 
     for load in loads[1:]:
@@ -170,6 +168,8 @@
                 dst[:, pl.ds(s * QUARTER, QUARTER)] = block
         for dst in places:
             dst[:, pl.ds(STACK, STRIDE - STACK)] = pad
+    across_1 = cross_plane(1)
+    halo_0 = halo(0, up, 0)
     for slot in (1, 2):
         shift_rows(slot, mine)
 

time: 54 us -> 55.1 us (1.020)
  Pallas kernels: 51 us -> 52.1 us
    pallas_call x1, Pallas kernels: 51 us -> 52.1 us  [local(): pl.pallas_call(kernel, out_shape=(jax.ShapeDtypeStruct((2, QUARTER, CELLS...]
where the time goes in v5:
time: 55.1 us; the launch traced here: 54.9 us
  Pallas kernels  52.1 us (95%)
  other arithmetic  1.43 us (3%)
  local copies, waits for them, and re-layouts  0.79 us (1%)
  between operations  0.64 us (1%)
    pallas_call x1, Pallas kernels, local(): pl.pallas_call(kernel, out_shape=(jax.ShapeDtypeStruct((2, QUARTER, CELLS...  52.1 us
    convert_element_type x1, other arithmetic, local(): return (grad_input, grad_weight[:27].astype(F32))  1.43 us

profile of v5, /device:TPU:0, one launch (start us, length us, event | category | flops | bytes accessed | tf_op | source)
XLA Modules:
  0.0 54.9 jit_solution(4873587465544028659)
XLA Ops:
  0.6 52.1 %shard_map.50 = (f32[2,64,1024]{2,1,0:T(8,128)S(1)}, bf16[28,64,256]{2,1,0:T(8,128)(2,1)S(1)}) custom-call(bf16[2,64,1024]{2,1,0:T(8,128)(2,1)} %f_ref.1, bf16[2,64,1024]{2,1,0:T(8,128)(2,1)} %cot_ref.1, bf16[3,576,256]{2,1,0:T(8,128)(2,1)} %bitcast.1), custom_call_target="tpu_custom_call" | custom-call | tf_op jit(solution)/shard_map/pallas_call | solution.py:410
  52.7 1.4 %slice_convert_fusion = f32[27,64,256]{2,1,0:T(8,128)} fusion(bf16[28,64,256]{2,1,0:T(8,128)(2,1)S(1)} %get-tuple-element.5), kind=kLoop, calls=%fused_computation | loop fusion | flops 442368 | bytes 2654208 | tf_op jit(solution)/shard_map/convert_element_type | solution.py:451
  54.2 0.8 %copy.6 = f32[2,64,1024]{2,1,0:T(8,128)} copy(f32[2,64,1024]{2,1,0:T(8,128)S(1)} %get-tuple-element.8) | data formatting | bytes 1048576

commit v6 on v3

--- a/solution.py
+++ b/solution.py
@@ -17,7 +17,7 @@
 BAND = 3 * QUARTER
 TILE = 256
 STRIDE = 640
-IN_TILE, OUT_TILE, D_TILE, ROWS = 256, 256, 256, 64
+IN_TILE, OUT_TILE, D_TILE, ROWS = 512, 512, 512, 64
 ROLL = BF16
 CHUNKS = ((0, 8, 2), (8, 8, 2), (16, 11, 3))
 SLOTS = 28

time: 54 us -> 54 us (level)
  no operation moved by 1% of the time
where the time goes in v6:
time: 54 us; the launch traced here: 53.9 us
  Pallas kernels  51 us (94%)
  other arithmetic  1.43 us (3%)
  local copies, waits for them, and re-layouts  0.79 us (1%)
  between operations  0.64 us (1%)
    pallas_call x1, Pallas kernels, local(): pl.pallas_call(kernel, out_shape=(jax.ShapeDtypeStruct((2, QUARTER, CELLS...  51 us
    convert_element_type x1, other arithmetic, local(): return (grad_input, grad_weight[:27].astype(F32))  1.43 us

profile of v6, /device:TPU:0, one launch (start us, length us, event | category | flops | bytes accessed | tf_op | source)
XLA Modules:
  0.0 53.9 jit_solution(12424453883145009018)
XLA Ops:
  0.6 51.0 %shard_map.50 = (f32[2,64,1024]{2,1,0:T(8,128)S(1)}, bf16[28,64,256]{2,1,0:T(8,128)(2,1)S(1)}) custom-call(bf16[2,64,1024]{2,1,0:T(8,128)(2,1)} %f_ref.1, bf16[2,64,1024]{2,1,0:T(8,128)(2,1)} %cot_ref.1, bf16[3,576,256]{2,1,0:T(8,128)(2,1)} %bitcast.1), custom_call_target="tpu_custom_call" | custom-call | tf_op jit(solution)/shard_map/pallas_call | solution.py:410
  51.7 1.4 %slice_convert_fusion = f32[27,64,256]{2,1,0:T(8,128)} fusion(bf16[28,64,256]{2,1,0:T(8,128)(2,1)S(1)} %get-tuple-element.5), kind=kLoop, calls=%fused_computation | loop fusion | flops 442368 | bytes 2654208 | tf_op jit(solution)/shard_map/convert_element_type | solution.py:451
  53.1 0.8 %copy.6 = f32[2,64,1024]{2,1,0:T(8,128)} copy(f32[2,64,1024]{2,1,0:T(8,128)S(1)} %get-tuple-element.8) | data formatting | bytes 1048576
